TPU v7x, 32 devices: a whole 2x2x4 slice. The times are simulated.
32 devices in a mesh: blk: 16 (over z, y, core), grp: 2 (over x).
Axes of the slice: x: 2, y: 2, z: 4, core: 2. Of those that a mesh axis runs over, the one named last changes fastest.
Arguments:
- left_env: bfloat16 [16, 24, 256, 256], P('blk', 'grp'), may hold values from -0.375 to 0.375
- right_env: bfloat16 [32, 24, 256, 256], P(('blk', 'grp')), may hold values from -0.078125 to 0.078125
- psi: bfloat16 [32, 1, 256, 256], P(('blk', 'grp')), may hold values from -6 to 6
- pairing: int32 [32, 1], P(('blk', 'grp')), may hold values from 0 to 15, as said below
- left_size: int32 [16], replicated, may hold values from 64 to 256, as said below
- right_size: int32 [32], P(('blk', 'grp')), may hold values from 64 to 256, as said below
Outputs:
- result: bfloat16 [32, 1, 256, 256], P(('blk', 'grp'))
Inputs may be any that keep to these rules, and one draw needn't show every extreme that they name: `pairing`: the 1 left sectors of one right sector are distinct. `left_size`: some left sector has exactly 256 live rows. `right_size`: some right sector has exactly 256 live columns.
All inputs are finite; a program needn't handle non-finite values.
Results may differ from a plain program's by a relative error of at most 0.005.
Values may be sent and summed in bfloat16 or wider, within the bound.
A program may use at most 64 MiB of HBM per device.

v0:
```python
import functools

import jax
import jax.numpy as jnp
from jax import lax
from jax.experimental import pallas as pl
from jax.experimental.pallas import tpu as pltpu
from jax.sharding import PartitionSpec as P

PLANE = 4
SLOTS = (3, 4, 5, 8)


def live_mask_of(shape, rows, cols):
    row = lax.broadcasted_iota(jnp.int32, shape, 0)
    col = lax.broadcasted_iota(jnp.int32, shape, 1)
    return (row < rows) & (col < cols)


def spread_kernel(
    planes, groups, pairing, left_env, table_out, own_out,
    table, lsend, lrecv, psend, precv, zsend, zrecv, local,
):
    members = PLANE * groups
    width = own_out.shape[1]
    blk, grp = lax.axis_index("blk"), lax.axis_index("grp")
    z, q = blk // PLANE, lax.rem(blk, PLANE)
    slot = q * groups + grp

    def peer(index):
        return {"blk": z * PLANE + index // groups, "grp": lax.rem(index, groups)}

    def level(index):
        return {"blk": index * PLANE + q, "grp": grp}

    barrier = pltpu.get_barrier_semaphore()
    for k in range(1, members):
        pl.semaphore_signal(barrier, inc=1, device_id=peer(lax.rem(slot + k, members)))
    for k in range(1, planes):
        pl.semaphore_signal(barrier, inc=1, device_id=level(lax.rem(z + k, planes)))

    left_own = pltpu.make_async_copy(left_env.at[0, pl.ds(q * width, width)], own_out.at[q], local)
    left_own.start()
    table[z, slot] = jnp.full(table.shape[2:], pairing[0, 0], jnp.int32)
    pl.semaphore_wait(barrier, members + planes - 2)

    def entry(k, to, where):
        return pltpu.make_async_remote_copy(
            src_ref=table.at[z, where], dst_ref=table.at[z, where], send_sem=psend.at[k],
            recv_sem=precv.at[k], device_id=peer(to))

    def column(k, to, where):
        return pltpu.make_async_remote_copy(
            src_ref=table.at[where], dst_ref=table.at[where], send_sem=zsend.at[k],
            recv_sem=zrecv.at[k], device_id=level(to))

    def left_copy(k, to, where):
        return pltpu.make_async_remote_copy(
            src_ref=left_env.at[0, pl.ds(to * width, width)], dst_ref=own_out.at[where],
            send_sem=lsend.at[k], recv_sem=lrecv.at[k],
            device_id={"blk": z * PLANE + to, "grp": grp})

    for k in range(1, members):
        entry(k, lax.rem(slot + k, members), slot).start()
    for k in range(1, PLANE):
        left_copy(k, lax.rem(q + k, PLANE), q).start()
    for k in range(1, members):
        back = lax.rem(slot + members - k, members)
        entry(k, back, back).wait_recv()
    for k in range(1, planes):
        column(k, lax.rem(z + k, planes), z).start()
    for k in range(1, planes):
        back = lax.rem(z + planes - k, planes)
        column(k, back, back).wait_recv()
    table_out[...] = table[...]
    for k in range(1, members):
        entry(k, lax.rem(slot + k, members), slot).wait_send()
    for k in range(1, planes):
        column(k, lax.rem(z + k, planes), z).wait_send()
    left_own.wait()
    for k in range(1, PLANE):
        back = lax.rem(q + PLANE - k, PLANE)
        left_copy(k, back, back).wait_recv()
        left_copy(k, lax.rem(q + k, PLANE), q).wait_send()


def apply_kernel(
    count, planes, groups, up_src, down_src, tile_at, own_size, psi, own, right_env, out,
    pool, staged, rights, psis, parts, arrived,
    msend, mrecv, rsend, rrecv, zsend, zrecv, psend, precv, local,
):
    members = PLANE * groups
    width = pool.shape[1]
    blk, grp = lax.axis_index("blk"), lax.axis_index("grp")
    z, q = blk // PLANE, lax.rem(blk, PLANE)
    slot = q * groups + grp
    half = right_env.shape[1] // groups
    has_below, has_above = z > 0, z < planes - 1

    def peer(index):
        return {"blk": z * PLANE + index // groups, "grp": lax.rem(index, groups)}

    barrier = pltpu.get_barrier_semaphore()

    @pl.loop(1, members)
    def _(k):
        pl.semaphore_signal(barrier, inc=1, device_id=peer(lax.rem(slot + k, members)))

    @pl.when(has_below)
    def _():
        pl.semaphore_signal(barrier, inc=1, device_id={"blk": blk - PLANE, "grp": grp})

    @pl.when(has_above)
    def _():
        pl.semaphore_signal(barrier, inc=1, device_id={"blk": blk + PLANE, "grp": grp})

    left_own = pltpu.make_async_copy(own, pool.at[pl.ds(0, PLANE)], local.at[0])
    right_own = pltpu.make_async_copy(
        right_env.at[0, pl.ds(grp * half + q * width, width)], rights.at[slot], local.at[1])
    left_own.start()
    right_own.start()
    live = live_mask_of(psi.shape[2:], own_size[0], own_size[1])
    psis[slot] = jnp.where(live, psi[0, 0].astype(jnp.float32), 0.0).astype(jnp.bfloat16)
    pl.semaphore_wait(barrier, members - 1 + has_below.astype(jnp.int32) + has_above.astype(jnp.int32))

    def tile_copy(k, to, where):
        return pltpu.make_async_remote_copy(
            src_ref=psis.at[where], dst_ref=psis.at[where], send_sem=msend.at[k],
            recv_sem=mrecv.at[k], device_id=peer(to))

    def right_copy(k, to, where):
        first = lax.rem(to, groups) * half + to // groups * width
        return pltpu.make_async_remote_copy(
            src_ref=right_env.at[0, pl.ds(first, width)], dst_ref=rights.at[where],
            send_sem=rsend.at[k], recv_sem=rrecv.at[k], device_id=peer(to))

    def start_plane():
        @pl.loop(1, members)
        def _(k):
            tile_copy(k, lax.rem(slot + k, members), slot).start()
            right_copy(k, lax.rem(slot + k, members), slot).start()

    left_own.wait()

    def z_copy(way, n, a):
        to = blk + PLANE if way == 0 else blk - PLANE
        return pltpu.make_async_remote_copy(
            src_ref=staged.at[way, n, a], dst_ref=pool.at[PLANE + way * count + n, a],
            send_sem=zsend.at[way, n, a], recv_sem=zrecv.at[way, n, a],
            device_id={"blk": to, "grp": grp})

    def forward(way, n, a, source, receives):
        first = PLANE + way * count
        at = source[n]
        if receives:
            z_copy(way, n, a).wait_recv()
        value = pool[0, a]
        for m in range(1, PLANE):
            value = jnp.where(at == m, pool[m, a], value)
        if receives:
            for m in range(n + 1):
                value = jnp.where(at == first + m, pool[first + m, a], value)
        staged[way, n, a] = value
        z_copy(way, n, a).start()

    for level in range(planes):
        @pl.when(z == level)
        def _():
            steps = []
            for i in range(count * width):
                if level < planes - 1:
                    steps.append((i + level, level, 0, i))
                if level > 0:
                    steps.append((i + planes - 1 - level, planes - 1 - level, 1, i))
            started = False
            for _, hops, way, i in sorted(steps):
                if hops > 0 and not started:
                    start_plane()
                    started = True
                source = up_src if way == 0 else down_src
                forward(way, i // width, i % width, source, hops > 0)
            if not started:
                start_plane()

    @pl.loop(1, members)
    def _(k):
        back = lax.rem(slot + members - k, members)
        tile_copy(k, back, back).wait_recv()
        right_copy(k, back, back).wait_recv()

    right_own.wait()
    for way, ends in ((0, planes - 1), (1, 0)):
        @pl.when(z == ends)
        def _():
            for n in range(count):
                for a in range(width):
                    z_copy(way, n, a).wait_recv()

    def part_copy(k, to):
        return pltpu.make_async_remote_copy(
            src_ref=parts.at[k], dst_ref=arrived.at[k], send_sem=psend.at[k],
            recv_sem=precv.at[k], device_id=peer(to))

    @pl.loop(1, members + 1)
    def _(k):
        t = lax.rem(slot + k, members)
        at = tile_at[t]
        tile = psis[t]
        total = jnp.zeros(tile.shape, jnp.float32)
        for a in range(width):
            inner = jnp.dot(pool[at, a], tile, preferred_element_type=jnp.float32)
            total += jnp.dot(inner.astype(jnp.bfloat16), rights[t, a], preferred_element_type=jnp.float32)
        parts[k] = total.astype(jnp.bfloat16)

        @pl.when(k < members)
        def _():
            part_copy(k, t).start()

    total = parts[members].astype(jnp.float32)
    for k in range(1, members):
        part_copy(k, lax.rem(slot + members - k, members)).wait_recv()
        total += arrived[k].astype(jnp.float32)
    out[0, 0] = jnp.where(live, total, 0.0).astype(jnp.bfloat16)

    @pl.loop(1, members)
    def _(k):
        tile_copy(k, lax.rem(slot + k, members), slot).wait_send()
        right_copy(k, lax.rem(slot + k, members), slot).wait_send()
        part_copy(k, lax.rem(slot + k, members)).wait_send()

    for way, sends in ((0, has_above), (1, has_below)):
        @pl.when(sends)
        def _():
            for n in range(count):
                for a in range(width):
                    z_copy(way, n, a).wait_send()


SMEM = pl.BlockSpec(memory_space=pltpu.SMEM)
VMEM = pl.BlockSpec(memory_space=pltpu.VMEM)
ANY = pl.BlockSpec(memory_space=pl.ANY)
DMA = pltpu.SemaphoreType.DMA


def apply_call(count, planes, groups, up_src, down_src, tile_at, own_size, psi, own, right_env):
    side = psi.shape[-1]
    members = PLANE * groups
    width = own.shape[1]
    return pl.pallas_call(
        functools.partial(apply_kernel, count, planes, groups),
        out_shape=jax.ShapeDtypeStruct((1, 1, side, side), jnp.bfloat16),
        in_specs=[SMEM] * 4 + [VMEM, ANY, ANY],
        out_specs=VMEM,
        scratch_shapes=[
            pltpu.VMEM((PLANE + 2 * count, width, side, side), jnp.bfloat16),
            pltpu.VMEM((2, count, width, side, side), jnp.bfloat16),
            pltpu.VMEM((members, width, side, side), jnp.bfloat16),
            pltpu.VMEM((members, side, side), jnp.bfloat16),
            pltpu.VMEM((members + 1, side, side), jnp.bfloat16),
            pltpu.VMEM((members, side, side), jnp.bfloat16),
            DMA((members,)), DMA((members,)), DMA((members,)), DMA((members,)),
            DMA((2, count, width)), DMA((2, count, width)), DMA((members,)), DMA((members,)),
            DMA((2,)),
        ],
        compiler_params=pltpu.CompilerParams(
            collective_id=count, has_side_effects=True, vmem_limit_bytes=48 * 1024 * 1024),
        name=f"apply_{count}",
    )(up_src, down_src, tile_at, own_size, psi, own, right_env)


def by_plane(left_env, right_env, psi, pairing, left_size, right_size):
    side = psi.shape[-1]
    groups = lax.axis_size("grp")
    blocks = lax.axis_size("blk")
    ranks, members, planes = blocks * groups, PLANE * groups, blocks // PLANE
    blk = lax.axis_index("blk")
    z = blk // PLANE
    width = left_env.shape[1] // PLANE
    table, own = pl.pallas_call(
        functools.partial(spread_kernel, planes, groups),
        out_shape=(
            jax.ShapeDtypeStruct((planes, members, 8, 128), jnp.int32),
            jax.ShapeDtypeStruct((PLANE, width, side, side), jnp.bfloat16),
        ),
        in_specs=[SMEM, ANY],
        out_specs=(VMEM, ANY),
        scratch_shapes=[
            pltpu.VMEM((planes, members, 8, 128), jnp.int32),
            DMA((PLANE,)), DMA((PLANE,)), DMA((members,)), DMA((members,)),
            DMA((planes,)), DMA((planes,)), DMA(()),
        ],
        compiler_params=pltpu.CompilerParams(collective_id=0, has_side_effects=True),
        name="spread",
    )(pairing, left_env)
    lefts = table[:, :, 0, 0].reshape(-1)
    sectors = jnp.arange(blocks)
    home = sectors // PLANE
    level = jnp.arange(planes)
    same = lefts[:, None] == sectors[None, :]
    tile_plane = jnp.arange(ranks) // members
    far_up = jnp.max(jnp.where(same, tile_plane[:, None], -1), axis=0)
    far_down = jnp.min(jnp.where(same, tile_plane[:, None], planes), axis=0)
    need_up = (home[None] <= level[:, None]) & (far_up[None] > level[:, None])
    need_down = (home[None] >= level[:, None]) & (far_down[None] < level[:, None])
    key_up, key_down = (planes - far_up) * blocks + sectors, far_down * blocks + sectors
    place_up = jnp.sum(need_up[:, None, :] & (key_up[None, None, :] < key_up[None, :, None]), axis=2)
    place_down = jnp.sum(need_down[:, None, :] & (key_down[None, None, :] < key_down[None, :, None]), axis=2)
    most = jnp.maximum(jnp.max(jnp.sum(need_up, axis=1)), jnp.max(jnp.sum(need_down, axis=1)))
    own_size = jnp.stack([
        jnp.sum(jnp.where(sectors == pairing[0, 0], left_size, 0)), right_size[0]])

    def row(array, index):
        return jnp.sum(jnp.where(level[:, None] == index, array, 0), axis=0)

    from_below, from_above = row(place_up, z - 1), row(place_down, z + 1)
    own_lefts = jnp.sum(
        jnp.where(jnp.arange(ranks)[None] == z * members + jnp.arange(members)[:, None], lefts[None], 0), axis=1)
    out_up, out_down = row(place_up, z), row(place_down, z)
    has_up, has_down = row(need_up.astype(jnp.int32), z), row(need_down.astype(jnp.int32), z)

    def run(count, *tensors):
        where = jnp.where(
            home == z, sectors - z * PLANE,
            jnp.where(home < z, PLANE + from_below, PLANE + count + from_above))
        slots = jnp.arange(count)[:, None]
        up_src = jnp.sum(jnp.where((has_up[None] > 0) & (out_up[None] == slots), where[None], 0), axis=1)
        down_src = jnp.sum(jnp.where((has_down[None] > 0) & (out_down[None] == slots), where[None], 0), axis=1)
        tile_at = jnp.sum(jnp.where(own_lefts[:, None] == sectors[None], where[None], 0), axis=1)
        return apply_call(count, planes, groups, up_src, down_src, tile_at, own_size, *tensors)

    choice = jnp.sum(most > jnp.array(SLOTS[:-1]))
    return lax.switch(
        choice, [functools.partial(run, count) for count in SLOTS], psi, own, right_env)


def per_device(left_env, right_env, psi, pairing, left_size, right_size):
    tile_side = psi.shape[-1]
    per_right = psi.shape[1]
    groups = lax.axis_size("grp")
    channels = left_env.shape[1]
    left_count = left_size.shape[0]
    cells = jnp.arange(tile_side)
    own_lefts = pairing[0]
    matches = own_lefts[:, None] == jnp.arange(left_count)[None, :]
    own_rows = jnp.sum(jnp.where(matches, left_size[None, :], 0), axis=1)
    row_mask = cells[None, :] < own_rows[:, None]
    column_mask = cells < right_size[0]
    live_mask = row_mask[:, :, None] & column_mask[None, None, :]
    masked = jnp.where(live_mask, psi[0], jnp.zeros((), jnp.bfloat16))
    all_tiles, all_lefts = (
        lax.all_gather(masked, "grp", axis=0, tiled=True),
        lax.all_gather(own_lefts, "grp", axis=0, tiled=True),
    )
    pair_count = all_tiles.shape[0]
    by_left = jnp.argsort(all_lefts, stable=True)
    ranked = all_lefts[by_left]
    initial = jnp.zeros((pair_count, tile_side, channels, tile_side), jnp.bfloat16)
    incoming = lax.all_gather(left_env, "blk", axis=0, tiled=True)
    first_row = jnp.int32(0)
    row_count = incoming.shape[0]
    lower_end = jnp.sum(ranked < first_row)
    upper_end = jnp.sum(ranked < first_row + row_count)

    def absorb_one(position, gathered):
        pair_slot = by_left[position]
        sector_slot = ranked[position] - first_row
        left_block = lax.dynamic_index_in_dim(incoming, sector_slot, 0, keepdims=False)
        psi_tile = lax.dynamic_index_in_dim(all_tiles, pair_slot, 0, keepdims=False)
        contracted = jnp.einsum(
            "alk,kr->lar", left_block, psi_tile, preferred_element_type=jnp.float32
        ).astype(jnp.bfloat16)
        return lax.dynamic_update_index_in_dim(gathered, contracted, pair_slot, 0)

    contracted_all = lax.fori_loop(lower_end, upper_end, absorb_one, initial)
    sectioned = contracted_all.reshape(groups, per_right, tile_side, channels, tile_side)
    right_flat = right_env[0].reshape(-1, tile_side)
    received = lax.all_to_all(sectioned, "grp", split_axis=0, concat_axis=3, tiled=True)
    item_count = received.shape[1]
    flattened = received.reshape(item_count * tile_side, -1)
    product = jnp.dot(flattened, right_flat, preferred_element_type=jnp.float32).reshape(
        item_count, tile_side, tile_side
    )
    result = jnp.where(live_mask, product, jnp.zeros((), jnp.float32)).astype(jnp.bfloat16)
    return result[None]


def apply(left_env, *rest):
    blocks, groups = lax.axis_size("blk"), lax.axis_size("grp")
    planes = blocks // PLANE
    most = max(min(PLANE * (p + 1), PLANE * groups * (planes - 1 - p)) for p in range(planes))
    single = left_env.shape[0] == 1 and rest[1].shape[1] == 1
    fits = single and blocks % PLANE == 0 and left_env.shape[1] % PLANE == 0 and most <= SLOTS[-1]
    return (by_plane if fits else per_device)(left_env, *rest)


def solution(mesh):
    return jax.shard_map(
        apply,
        mesh=mesh,
        in_specs=(
            P("blk", "grp", None, None),
            P(("blk", "grp"), None, None, None),
            P(("blk", "grp"), None, None, None),
            P(("blk", "grp"), None),
            P(),
            P(("blk", "grp")),
        ),
        out_specs=P(("blk", "grp"), None, None, None),
        check_vma=False,
    )
```

profile of v0, /device:TPU:0, one launch (start us, length us, event | category | flops | bytes accessed | tf_op | source)
XLA Modules:
  0.0 100.4 jit_solution(166894252293739888)
XLA Ops:
  0.0 0.0 copy-start.1
  0.0 0.0 copy-start
  1.3 1.4 %fusion.11 = s32[]{:T(128)} fusion(s32[16]{0:T(128)} %param.15, s32[]{:T(128)} %bitcast.2), kind=kLoop, calls=%fused_computation.111 | loop fusion | flops 47 | bytes 72 | tf_op jit(solution)/shard_map/reduce_sum | solution.py:310
  2.7 0.8 pad_add_fusion
  3.5 0.1 broadcast_in_dim.230
  3.6 23.5 %spread.1 = (s32[4,8,8,128]{3,2,1,0:T(8,128)}, bf16[4,3,256,256]{3,2,1,0:T(8,128)(2,1)S(1)}) custom-call(s32[1,1]{1,0:T(1,128)} %copy.37.pairing, bf16[1,12,256,256]{3,2,1,0:T(8,128)(2,1)} %left_env.1), custom_call_target="tpu_custom_call" | custom-call | tf_op jit(solution)/shard_map/spread/pallas_call | solution.py:279
  27.1 1.6 %slice_reduce_fusion = s32[4,8]{1,0:T(4,128)S(1)} fusion(s32[4,8,8,128]{3,2,1,0:T(8,128)} %get-tuple-element.196), kind=kLoop, calls=%fused_computation.86 | loop fusion | bytes 256 | tf_op jit(solution)/shard_map/slice | solution.py:295
  28.7 0.1 eq.253
  28.8 0.1 select_reduce_fusion.40
  28.9 0.1 broadcast_compare_fusion.16
  29.0 0.1 broadcast_compare_fusion.17
  29.1 0.1 convert_reduce_fusion
  29.2 0.1 convert_reduce_fusion.1
  29.4 0.1 convert_reduce_fusion.2
  29.5 0.6 reduce_max.28
  30.2 0.7 reduce_max.29
  32.2 0.0 copy-done.1
  32.2 0.6 fusion.10
  32.9 0.0 copy-done
  33.5 66.2 %conditional.1 = (bf16[1,1,256,256]{3,2,1,0:T(8,128)(2,1)S(1)}) conditional(s32[]{:T(128)} %clamp.3, (pred[4,16]{1,0:T(4,128)(4,1)S(1)}, pred[4,16]{1,0:T(4,128)(4,1)S(1)}, s32[]{:T(128)}, s32[16]{0:T(128)S(1)}, s32[16]{0:T(128)S(1)}, /*index=5*/s32[16]{0:T(128)S(1)}, s32[4]{0:T(128)S(1)}, s32[4]{0:T(128)S(1)}, ...), branch_computations={%region_17.21_spmd.clone, %region_21.25_spmd.clone, %region_25.29_... | conditional | flops 2980 | bytes 4336 | solution.py:332
  33.6 0.2 select_reduce_fusion.10
  33.8 0.1 select_reduce_fusion.12
  33.9 0.2 select_reduce_fusion.11.tile_at
  34.1 0.1 select_reduce_fusion.18
  34.2 65.3 %apply_4.1 = bf16[1,1,256,256]{3,2,1,0:T(8,128)(2,1)S(1)} custom-call(s32[4]{0:T(128)S(1)} %get-tuple-element.754.up_src, s32[4]{0:T(128)S(1)} %get-tuple-element.753.down_src, s32[8]{0:T(128)S(1)} %select_reduce_fusion.11.tile_at, s32[2]{0:T(128)S(1)} %get-tuple-element.521.own_size, bf16[1,1,256,256]{3,2,1,0:T(8,128)(2,1)S(1)} %get-tuple-element.546.psi, ...), custom_call_target="tpu_custom_call" | custom-call | tf_op jit(solution)/shard_map/cond/branch_1_fun/apply_4/pallas_call | solution.py:249
  99.8 0.7 copy.39
  (15 shorter events, 0.1 us)
Async XLA Ops:
  0.0 32.2 %copy-start.1 = (s32[3]{0:T(128)S(1)}, s32[3]{0:T(128)}, u32[]{:S(2)}) copy-start(s32[3]{0:T(128)} %constant.97.clone) | copy-start | bytes 40
  0.0 32.9 %copy-start = (bf16[1,1,256,256]{3,2,1,0:T(8,128)(2,1)S(1)}, bf16[1,1,256,256]{3,2,1,0:T(8,128)(2,1)}, u32[]{:S(2)}) copy-start(bf16[1,1,256,256]{3,2,1,0:T(8,128)(2,1)} %param.13) | copy-start | bytes 393220
where the time goes:
time: 101 us; the launch traced here: 100 us
  Pallas kernels  88.8 us (88%)
  other arithmetic  5.5 us (5%)
  between operations  3.4 us (3%)
  local copies, waits for them, and re-layouts  2.4 us (2%)
    pallas_call x1, Pallas kernels, apply_call(): pl.pallas_call(functools.partial(apply_kernel, count, planes, groups), ou...  65.3 us
    pallas_call x1, Pallas kernels, by_plane(): pl.pallas_call(functools.partial(spread_kernel, planes, groups), out_shap...  23.5 us

commit v1 on v0

--- a/solution.py
+++ b/solution.py
@@ -85,9 +85,9 @@
 
 
 def apply_kernel(
-    count, planes, groups, up_src, down_src, tile_at, own_size, psi, own, right_env, out,
-    pool, staged, rights, psis, parts, arrived,
-    msend, mrecv, rsend, rrecv, zsend, zrecv, psend, precv, local,
+    count, planes, groups, up_src, down_src, tile_at, pairing, left_size, right_size, psi, own, right_env, out,
+    pool, staged, rights, psis, given, taken, kept, joined, arrived,
+    msend, mrecv, rsend, rrecv, zsend, zrecv, gsend, grecv, psend, precv, local,
 ):
     members = PLANE * groups
     width = pool.shape[1]
@@ -96,6 +96,13 @@
     slot = q * groups + grp
     half = right_env.shape[1] // groups
     has_below, has_above = z > 0, z < planes - 1
+    chips = members // 2
+    core, chip = lax.rem(q, 2), q // 2 * groups + grp
+
+    def member(on_chip, on_core):
+        return (on_chip // groups * 2 + on_core) * groups + lax.rem(on_chip, groups)
+
+    sibling = member(chip, 1 - core)
 
     def peer(index):
         return {"blk": z * PLANE + index // groups, "grp": lax.rem(index, groups)}
@@ -119,7 +126,7 @@
         right_env.at[0, pl.ds(grp * half + q * width, width)], rights.at[slot], local.at[1])
     left_own.start()
     right_own.start()
-    live = live_mask_of(psi.shape[2:], own_size[0], own_size[1])
+    live = live_mask_of(psi.shape[2:], left_size[pairing[0, 0]], right_size[0])
     psis[slot] = jnp.where(live, psi[0, 0].astype(jnp.float32), 0.0).astype(jnp.bfloat16)
     pl.semaphore_wait(barrier, members - 1 + has_below.astype(jnp.int32) + has_above.astype(jnp.int32))
 
@@ -135,9 +142,14 @@
             send_sem=rsend.at[k], recv_sem=rrecv.at[k], device_id=peer(to))
 
     def start_plane():
+        @pl.loop(1, chips)
+        def _(d):
+            tile_copy(d, member(lax.rem(chip + d, chips), core), slot).start()
+
+        tile_copy(0, sibling, slot).start()
+
         @pl.loop(1, members)
         def _(k):
-            tile_copy(k, lax.rem(slot + k, members), slot).start()
             right_copy(k, lax.rem(slot + k, members), slot).start()
 
     left_own.wait()
@@ -182,11 +194,18 @@
             if not started:
                 start_plane()
 
-    @pl.loop(1, members)
-    def _(k):
-        back = lax.rem(slot + members - k, members)
-        tile_copy(k, back, back).wait_recv()
-        right_copy(k, back, back).wait_recv()
+    @pl.loop(1, chips)
+    def _(d):
+        came = member(lax.rem(chip + chips - d, chips), core)
+        tile_copy(d, came, came).wait_recv()
+        tile_copy(chips + d, sibling, came).start()
+
+    tile_copy(0, sibling, sibling).wait_recv()
+
+    @pl.loop(1, chips)
+    def _(d):
+        came = member(lax.rem(chip + chips - d, chips), 1 - core)
+        tile_copy(chips + d, sibling, came).wait_recv()
 
     right_own.wait()
     for way, ends in ((0, planes - 1), (1, 0)):
@@ -196,37 +215,75 @@
                 for a in range(width):
                     z_copy(way, n, a).wait_recv()
 
-    def part_copy(k, to):
-        return pltpu.make_async_remote_copy(
-            src_ref=parts.at[k], dst_ref=arrived.at[k], send_sem=psend.at[k],
-            recv_sem=precv.at[k], device_id=peer(to))
-
-    @pl.loop(1, members + 1)
-    def _(k):
-        t = lax.rem(slot + k, members)
+    def give_copy(d):
+        return pltpu.make_async_remote_copy(
+            src_ref=given.at[d], dst_ref=taken.at[d], send_sem=gsend.at[d],
+            recv_sem=grecv.at[d], device_id=peer(sibling))
+
+    def part_copy(d, to):
+        return pltpu.make_async_remote_copy(
+            src_ref=joined.at[d], dst_ref=arrived.at[d], send_sem=psend.at[d],
+            recv_sem=precv.at[d], device_id=peer(to))
+
+    def contract(t):
         at = tile_at[t]
         tile = psis[t]
         total = jnp.zeros(tile.shape, jnp.float32)
         for a in range(width):
             inner = jnp.dot(pool[at, a], tile, preferred_element_type=jnp.float32)
             total += jnp.dot(inner.astype(jnp.bfloat16), rights[t, a], preferred_element_type=jnp.float32)
-        parts[k] = total.astype(jnp.bfloat16)
-
-        @pl.when(k < members)
+        return total
+
+    def wait_right(t):
+        right_copy(lax.rem(slot + members - t, members), t, t).wait_recv()
+
+    def join(d):
+        give_copy(d).wait_recv()
+        joined[d] = (kept[d] + taken[d].astype(jnp.float32)).astype(jnp.bfloat16)
+        part_copy(d, member(lax.rem(chip + d, chips), core)).start()
+
+    @pl.loop(1, chips + 1)
+    def _(d):
+        there = lax.rem(chip + d, chips)
+        theirs, mine = member(there, 1 - core), member(there, core)
+        wait_right(theirs)
+        given[d] = contract(theirs).astype(jnp.bfloat16)
+        give_copy(d).start()
+
+        @pl.when(d < chips)
         def _():
-            part_copy(k, t).start()
-
-    total = parts[members].astype(jnp.float32)
-    for k in range(1, members):
-        part_copy(k, lax.rem(slot + members - k, members)).wait_recv()
-        total += arrived[k].astype(jnp.float32)
+            wait_right(mine)
+
+        kept[d] = contract(mine)
+
+        @pl.when(d > 1)
+        def _():
+            join(d - 1)
+
+    give_copy(chips).wait_recv()
+    total = kept[chips] + taken[chips].astype(jnp.float32)
+    for d in range(1, chips):
+        part_copy(d, member(lax.rem(chip + chips - d, chips), core)).wait_recv()
+        total += arrived[d].astype(jnp.float32)
     out[0, 0] = jnp.where(live, total, 0.0).astype(jnp.bfloat16)
 
     @pl.loop(1, members)
     def _(k):
-        tile_copy(k, lax.rem(slot + k, members), slot).wait_send()
         right_copy(k, lax.rem(slot + k, members), slot).wait_send()
-        part_copy(k, lax.rem(slot + k, members)).wait_send()
+
+    tile_copy(0, sibling, slot).wait_send()
+
+    @pl.loop(1, chips)
+    def _(d):
+        to = member(lax.rem(chip + d, chips), core)
+        tile_copy(d, to, slot).wait_send()
+        came = member(lax.rem(chip + chips - d, chips), core)
+        tile_copy(chips + d, sibling, came).wait_send()
+        part_copy(d, to).wait_send()
+
+    @pl.loop(1, chips + 1)
+    def _(d):
+        give_copy(d).wait_send()
 
     for way, sends in ((0, has_above), (1, has_below)):
         @pl.when(sends)
@@ -242,30 +299,34 @@
 DMA = pltpu.SemaphoreType.DMA
 
 
-def apply_call(count, planes, groups, up_src, down_src, tile_at, own_size, psi, own, right_env):
+def apply_call(count, planes, groups, up_src, down_src, tile_at, pairing, left_size, right_size, psi, own, right_env):
     side = psi.shape[-1]
     members = PLANE * groups
-    width = own.shape[1]
+    width, chips = own.shape[1], members // 2
     return pl.pallas_call(
         functools.partial(apply_kernel, count, planes, groups),
         out_shape=jax.ShapeDtypeStruct((1, 1, side, side), jnp.bfloat16),
-        in_specs=[SMEM] * 4 + [VMEM, ANY, ANY],
+        in_specs=[SMEM] * 6 + [VMEM, ANY, ANY],
         out_specs=VMEM,
         scratch_shapes=[
             pltpu.VMEM((PLANE + 2 * count, width, side, side), jnp.bfloat16),
             pltpu.VMEM((2, count, width, side, side), jnp.bfloat16),
             pltpu.VMEM((members, width, side, side), jnp.bfloat16),
             pltpu.VMEM((members, side, side), jnp.bfloat16),
-            pltpu.VMEM((members + 1, side, side), jnp.bfloat16),
-            pltpu.VMEM((members, side, side), jnp.bfloat16),
-            DMA((members,)), DMA((members,)), DMA((members,)), DMA((members,)),
-            DMA((2, count, width)), DMA((2, count, width)), DMA((members,)), DMA((members,)),
+            pltpu.VMEM((chips + 1, side, side), jnp.bfloat16),
+            pltpu.VMEM((chips + 1, side, side), jnp.bfloat16),
+            pltpu.VMEM((chips + 1, side, side), jnp.float32),
+            pltpu.VMEM((chips, side, side), jnp.bfloat16),
+            pltpu.VMEM((chips, side, side), jnp.bfloat16),
+            DMA((2 * chips,)), DMA((2 * chips,)), DMA((members,)), DMA((members,)),
+            DMA((2, count, width)), DMA((2, count, width)), DMA((chips + 1,)), DMA((chips + 1,)),
+            DMA((chips,)), DMA((chips,)),
             DMA((2,)),
         ],
         compiler_params=pltpu.CompilerParams(
             collective_id=count, has_side_effects=True, vmem_limit_bytes=48 * 1024 * 1024),
         name=f"apply_{count}",
-    )(up_src, down_src, tile_at, own_size, psi, own, right_env)
+    )(up_src, down_src, tile_at, pairing, left_size, right_size, psi, own, right_env)
 
 
 def by_plane(left_env, right_env, psi, pairing, left_size, right_size):
@@ -306,9 +367,6 @@
     place_up = jnp.sum(need_up[:, None, :] & (key_up[None, None, :] < key_up[None, :, None]), axis=2)
     place_down = jnp.sum(need_down[:, None, :] & (key_down[None, None, :] < key_down[None, :, None]), axis=2)
     most = jnp.maximum(jnp.max(jnp.sum(need_up, axis=1)), jnp.max(jnp.sum(need_down, axis=1)))
-    own_size = jnp.stack([
-        jnp.sum(jnp.where(sectors == pairing[0, 0], left_size, 0)), right_size[0]])
-
     def row(array, index):
         return jnp.sum(jnp.where(level[:, None] == index, array, 0), axis=0)
 
@@ -318,7 +376,7 @@
     out_up, out_down = row(place_up, z), row(place_down, z)
     has_up, has_down = row(need_up.astype(jnp.int32), z), row(need_down.astype(jnp.int32), z)
 
-    def run(count, *tensors):
+    def run(count, *operands):
         where = jnp.where(
             home == z, sectors - z * PLANE,
             jnp.where(home < z, PLANE + from_below, PLANE + count + from_above))
@@ -326,11 +384,12 @@
         up_src = jnp.sum(jnp.where((has_up[None] > 0) & (out_up[None] == slots), where[None], 0), axis=1)
         down_src = jnp.sum(jnp.where((has_down[None] > 0) & (out_down[None] == slots), where[None], 0), axis=1)
         tile_at = jnp.sum(jnp.where(own_lefts[:, None] == sectors[None], where[None], 0), axis=1)
-        return apply_call(count, planes, groups, up_src, down_src, tile_at, own_size, *tensors)
+        return apply_call(count, planes, groups, up_src, down_src, tile_at, *operands)
 
     choice = jnp.sum(most > jnp.array(SLOTS[:-1]))
     return lax.switch(
-        choice, [functools.partial(run, count) for count in SLOTS], psi, own, right_env)
+        choice, [functools.partial(run, count) for count in SLOTS],
+        pairing, left_size, right_size, psi, own, right_env)
 
 
 def per_device(left_env, right_env, psi, pairing, left_size, right_size):

time: 101 us -> 91.5 us (0.906); the launches traced: 100 us -> 89.8 us
  Pallas kernels: 88.8 us -> 81 us
  other arithmetic: 5.5 us -> 3.36 us
    pallas_call x1, Pallas kernels: 65.3 us -> 57.5 us  [apply_call(): pl.pallas_call(functools.partial(apply_kernel, count, planes, groups), ou...]
    reduce_sum x1 -> x0, other arithmetic: 1.37 us -> none  [by_plane(): jnp.sum(jnp.where(sectors == pairing[0, 0], left_size, 0))]
where the time goes in v1:
time: 91.5 us; the launch traced here: 89.8 us
  Pallas kernels  81 us (89%)
  other arithmetic  3.36 us (4%)
  between operations  2.77 us (3%)
  local copies, waits for them, and re-layouts  2.4 us (3%)
    pallas_call x1, Pallas kernels, apply_call(): pl.pallas_call(functools.partial(apply_kernel, count, planes, groups), ou...  57.5 us
    pallas_call x1, Pallas kernels, by_plane(): pl.pallas_call(functools.partial(spread_kernel, planes, groups), out_shap...  23.6 us

profile of v1, /device:TPU:0, one launch (start us, length us, event | category | flops | bytes accessed | tf_op | source)
XLA Modules:
  0.0 89.8 jit_solution(17761301022291574571)
XLA Ops:
  0.0 0.0 copy-start.2
  0.0 0.0 copy-start.1
  0.0 0.0 copy-start
  0.7 0.1 broadcast_in_dim.228
  0.8 23.6 %spread.1 = (s32[4,8,8,128]{3,2,1,0:T(8,128)}, bf16[4,3,256,256]{3,2,1,0:T(8,128)(2,1)S(1)}) custom-call(s32[1,1]{1,0:T(1,128)S(6)} %copy.53.pairing, bf16[1,12,256,256]{3,2,1,0:T(8,128)(2,1)} %left_env.1), custom_call_target="tpu_custom_call" | custom-call | tf_op jit(solution)/shard_map/spread/pallas_call | solution.py:340
  24.4 1.6 %slice_reduce_fusion = s32[4,8]{1,0:T(4,128)S(1)} fusion(s32[4,8,8,128]{3,2,1,0:T(8,128)} %get-tuple-element.220), kind=kLoop, calls=%fused_computation.86 | loop fusion | bytes 256 | tf_op jit(solution)/shard_map/slice | solution.py:356
  25.9 0.1 eq.247
  26.0 0.1 select_reduce_fusion.40
  26.2 0.1 broadcast_compare_fusion.16
  26.2 0.1 broadcast_compare_fusion.17
  26.3 0.1 convert_reduce_fusion
  26.5 0.1 convert_reduce_fusion.1
  26.6 0.1 convert_reduce_fusion.2
  26.8 0.6 reduce_max.28
  27.4 0.7 reduce_max.29
  29.5 0.0 copy-done.2
  29.5 0.6 fusion.10
  30.1 0.0 copy-done.1
  30.1 0.0 copy-done
  30.8 58.4 %conditional.1 = (bf16[1,1,256,256]{3,2,1,0:T(8,128)(2,1)S(1)}) conditional(s32[]{:T(128)} %clamp.3, (pred[4,16]{1,0:T(4,128)(4,1)S(1)}, pred[4,16]{1,0:T(4,128)(4,1)S(1)}, s32[]{:T(128)}, s32[16]{0:T(128)S(1)}, s32[16]{0:T(128)S(1)}, /*index=5*/s32[16]{0:T(128)S(1)}, s32[4]{0:T(128)S(1)}, s32[4]{0:T(128)S(1)}, ...), branch_computations={%region_16.20_spmd.clone, %region_20.24_spmd.clone, %region_24.28_... | conditional | flops 2980 | bytes 4336 | solution.py:390
  30.8 0.2 select_reduce_fusion
  31.0 0.1 select_reduce_fusion.2
  31.1 0.2 select_reduce_fusion.1.tile_at
  31.3 0.1 select_reduce_fusion.8
  31.5 57.5 %apply_3.1 = bf16[1,1,256,256]{3,2,1,0:T(8,128)(2,1)S(1)} custom-call(s32[3]{0:T(128)S(1)} %get-tuple-element.800.up_src, s32[3]{0:T(128)S(1)} %get-tuple-element.799.down_src, s32[8]{0:T(128)S(1)} %select_reduce_fusion.1.tile_at, s32[1,1]{1,0:T(1,128)} %get-tuple-element.488.pairing, s32[16]{0:T(128)S(1)} %get-tuple-element.513.left_size, ...), custom_call_target="tpu_custom_call" | custom-call | tf_op jit(solution)/shard_map/cond/branch_0_fun/apply_3/pallas_call | solution.py:306
  89.2 0.7 copy.54
  (15 shorter events, 0.1 us)
Async XLA Ops:
  0.0 29.5 %copy-start.2 = (s32[3]{0:T(128)S(1)}, s32[3]{0:T(128)}, u32[]{:S(2)}) copy-start(s32[3]{0:T(128)} %constant.97.clone) | copy-start | bytes 40
  0.0 30.1 %copy-start.1 = (s32[16]{0:T(128)S(1)}, s32[16]{0:T(128)}, u32[]{:S(2)}) copy-start(s32[16]{0:T(128)} %param.15) | copy-start | bytes 196
  0.0 30.1 %copy-start = (bf16[1,1,256,256]{3,2,1,0:T(8,128)(2,1)S(1)}, bf16[1,1,256,256]{3,2,1,0:T(8,128)(2,1)}, u32[]{:S(2)}) copy-start(bf16[1,1,256,256]{3,2,1,0:T(8,128)(2,1)} %param.13) | copy-start | bytes 393220

commit v2 on v1

--- a/solution.py
+++ b/solution.py
@@ -8,6 +8,7 @@
 from jax.sharding import PartitionSpec as P
 
 PLANE = 4
+ABOVE = 64
 SLOTS = (3, 4, 5, 8)
 
 
@@ -17,8 +18,66 @@
     return (row < rows) & (col < cols)
 
 
+def plan_of(planes, groups, z, table):
+    members, blocks = PLANE * groups, planes * PLANE
+    shape = (blocks, 128)
+    sub = lax.broadcasted_iota(jnp.int32, shape, 0)
+    lane = lax.broadcasted_iota(jnp.int32, shape, 1)
+
+    def spread(value):
+        return jnp.broadcast_to(value[:1], shape)
+
+    def facts(sector):
+        up, down = jnp.full(shape, -1, jnp.int32), jnp.full(shape, planes, jnp.int32)
+        for p in range(planes):
+            here = jnp.zeros(shape, jnp.int32)
+            for t in range(members):
+                here = jnp.where(spread(table[p, t]) == sector, 1, here)
+            up = jnp.where(here > 0, p, up)
+            down = jnp.where((here > 0) & (down == planes), p, down)
+        home = sector // PLANE
+        return home, up, down, (planes - up) * blocks + sector, down * blocks + sector
+
+    home_s, up_s, down_s, key_up_s, key_down_s = facts(sub)
+    home_l, up_l, down_l, key_up_l, key_down_l = facts(lane)
+
+    def need(home, far, p, upward):
+        return (home <= p) & (far > p) if upward else (home >= p) & (far < p)
+
+    def place(p, upward):
+        keys, mine = (key_up_l, key_up_s) if upward else (key_down_l, key_down_s)
+        before = need(home_l, up_l if upward else down_l, p, upward) & (keys < mine)
+        count = jnp.sum(jnp.where(before, 1.0, 0.0), axis=1, keepdims=True)
+        return jnp.broadcast_to(count, shape).astype(jnp.int32)
+
+    where = jnp.where(
+        home_s == z, sub - z * PLANE,
+        jnp.where(home_s < z, PLANE + place(z - 1, True), ABOVE + place(z + 1, False)))
+
+    def total(values):
+        return jnp.sum(values.astype(jnp.float32), axis=0, keepdims=True).astype(jnp.int32)
+
+    def sources(upward):
+        out = need(home_s, up_s if upward else down_s, z, upward) & (place(z, upward) == lane)
+        return total(jnp.where(out, where, 0))
+
+    lefts = jnp.full(shape, -1, jnp.int32)
+    for t in range(members):
+        lefts = jnp.where(lane == t, spread(table[z, t]), lefts)
+    most = jnp.zeros((1, 128), jnp.int32)
+    for p in range(planes):
+        most = jnp.maximum(most, total(jnp.where(need(home_s, up_s, p, True), 1, 0)))
+        most = jnp.maximum(most, total(jnp.where(need(home_s, down_s, p, False), 1, 0)))
+    rows = (sources(True), sources(False), total(jnp.where(lefts == sub, where, 0)), most)
+    out = jnp.zeros((8, 128), jnp.int32)
+    row = lax.broadcasted_iota(jnp.int32, out.shape, 0)
+    for index, value in enumerate(rows):
+        out = jnp.where(row == index, jnp.broadcast_to(value, out.shape), out)
+    return out
+
+
 def spread_kernel(
-    planes, groups, pairing, left_env, table_out, own_out,
+    planes, groups, pairing, left_env, plan_out, own_out,
     table, lsend, lrecv, psend, precv, zsend, zrecv, local,
 ):
     members = PLANE * groups
@@ -72,7 +131,7 @@
     for k in range(1, planes):
         back = lax.rem(z + planes - k, planes)
         column(k, back, back).wait_recv()
-    table_out[...] = table[...]
+    plan_out[...] = plan_of(planes, groups, z, table)
     for k in range(1, members):
         entry(k, lax.rem(slot + k, members), slot).wait_send()
     for k in range(1, planes):
@@ -85,7 +144,7 @@
 
 
 def apply_kernel(
-    count, planes, groups, up_src, down_src, tile_at, pairing, left_size, right_size, psi, own, right_env, out,
+    count, planes, groups, plan, pairing, left_size, right_size, psi, own, right_env, out,
     pool, staged, rights, psis, given, taken, kept, joined, arrived,
     msend, mrecv, rsend, rrecv, zsend, zrecv, gsend, grecv, psend, precv, local,
 ):
@@ -161,9 +220,12 @@
             send_sem=zsend.at[way, n, a], recv_sem=zrecv.at[way, n, a],
             device_id={"blk": to, "grp": grp})
 
-    def forward(way, n, a, source, receives):
+    def placed(at):
+        return jnp.where(at >= ABOVE, at - ABOVE + PLANE + count, at)
+
+    def forward(way, n, a, receives):
         first = PLANE + way * count
-        at = source[n]
+        at = placed(plan[way, n])
         if receives:
             z_copy(way, n, a).wait_recv()
         value = pool[0, a]
@@ -189,8 +251,7 @@
                 if hops > 0 and not started:
                     start_plane()
                     started = True
-                source = up_src if way == 0 else down_src
-                forward(way, i // width, i % width, source, hops > 0)
+                forward(way, i // width, i % width, hops > 0)
             if not started:
                 start_plane()
 
@@ -226,7 +287,7 @@
             recv_sem=precv.at[d], device_id=peer(to))
 
     def contract(t):
-        at = tile_at[t]
+        at = placed(plan[2, t])
         tile = psis[t]
         total = jnp.zeros(tile.shape, jnp.float32)
         for a in range(width):
@@ -299,14 +360,14 @@
 DMA = pltpu.SemaphoreType.DMA
 
 
-def apply_call(count, planes, groups, up_src, down_src, tile_at, pairing, left_size, right_size, psi, own, right_env):
+def apply_call(count, planes, groups, plan, pairing, left_size, right_size, psi, own, right_env):
     side = psi.shape[-1]
     members = PLANE * groups
     width, chips = own.shape[1], members // 2
     return pl.pallas_call(
         functools.partial(apply_kernel, count, planes, groups),
         out_shape=jax.ShapeDtypeStruct((1, 1, side, side), jnp.bfloat16),
-        in_specs=[SMEM] * 6 + [VMEM, ANY, ANY],
+        in_specs=[SMEM] * 4 + [VMEM, ANY, ANY],
         out_specs=VMEM,
         scratch_shapes=[
             pltpu.VMEM((PLANE + 2 * count, width, side, side), jnp.bfloat16),
@@ -326,21 +387,19 @@
         compiler_params=pltpu.CompilerParams(
             collective_id=count, has_side_effects=True, vmem_limit_bytes=48 * 1024 * 1024),
         name=f"apply_{count}",
-    )(up_src, down_src, tile_at, pairing, left_size, right_size, psi, own, right_env)
+    )(plan, pairing, left_size, right_size, psi, own, right_env)
 
 
 def by_plane(left_env, right_env, psi, pairing, left_size, right_size):
     side = psi.shape[-1]
     groups = lax.axis_size("grp")
     blocks = lax.axis_size("blk")
-    ranks, members, planes = blocks * groups, PLANE * groups, blocks // PLANE
-    blk = lax.axis_index("blk")
-    z = blk // PLANE
+    members, planes = PLANE * groups, blocks // PLANE
     width = left_env.shape[1] // PLANE
-    table, own = pl.pallas_call(
+    plan, own = pl.pallas_call(
         functools.partial(spread_kernel, planes, groups),
         out_shape=(
-            jax.ShapeDtypeStruct((planes, members, 8, 128), jnp.int32),
+            jax.ShapeDtypeStruct((8, 128), jnp.int32),
             jax.ShapeDtypeStruct((PLANE, width, side, side), jnp.bfloat16),
         ),
         in_specs=[SMEM, ANY],
@@ -353,43 +412,12 @@
         compiler_params=pltpu.CompilerParams(collective_id=0, has_side_effects=True),
         name="spread",
     )(pairing, left_env)
-    lefts = table[:, :, 0, 0].reshape(-1)
-    sectors = jnp.arange(blocks)
-    home = sectors // PLANE
-    level = jnp.arange(planes)
-    same = lefts[:, None] == sectors[None, :]
-    tile_plane = jnp.arange(ranks) // members
-    far_up = jnp.max(jnp.where(same, tile_plane[:, None], -1), axis=0)
-    far_down = jnp.min(jnp.where(same, tile_plane[:, None], planes), axis=0)
-    need_up = (home[None] <= level[:, None]) & (far_up[None] > level[:, None])
-    need_down = (home[None] >= level[:, None]) & (far_down[None] < level[:, None])
-    key_up, key_down = (planes - far_up) * blocks + sectors, far_down * blocks + sectors
-    place_up = jnp.sum(need_up[:, None, :] & (key_up[None, None, :] < key_up[None, :, None]), axis=2)
-    place_down = jnp.sum(need_down[:, None, :] & (key_down[None, None, :] < key_down[None, :, None]), axis=2)
-    most = jnp.maximum(jnp.max(jnp.sum(need_up, axis=1)), jnp.max(jnp.sum(need_down, axis=1)))
-    def row(array, index):
-        return jnp.sum(jnp.where(level[:, None] == index, array, 0), axis=0)
-
-    from_below, from_above = row(place_up, z - 1), row(place_down, z + 1)
-    own_lefts = jnp.sum(
-        jnp.where(jnp.arange(ranks)[None] == z * members + jnp.arange(members)[:, None], lefts[None], 0), axis=1)
-    out_up, out_down = row(place_up, z), row(place_down, z)
-    has_up, has_down = row(need_up.astype(jnp.int32), z), row(need_down.astype(jnp.int32), z)
-
-    def run(count, *operands):
-        where = jnp.where(
-            home == z, sectors - z * PLANE,
-            jnp.where(home < z, PLANE + from_below, PLANE + count + from_above))
-        slots = jnp.arange(count)[:, None]
-        up_src = jnp.sum(jnp.where((has_up[None] > 0) & (out_up[None] == slots), where[None], 0), axis=1)
-        down_src = jnp.sum(jnp.where((has_down[None] > 0) & (out_down[None] == slots), where[None], 0), axis=1)
-        tile_at = jnp.sum(jnp.where(own_lefts[:, None] == sectors[None], where[None], 0), axis=1)
-        return apply_call(count, planes, groups, up_src, down_src, tile_at, *operands)
-
-    choice = jnp.sum(most > jnp.array(SLOTS[:-1]))
+    choice = jnp.int32(0)
+    for count in SLOTS[:-1]:
+        choice += (plan[3, 0] > count).astype(jnp.int32)
     return lax.switch(
-        choice, [functools.partial(run, count) for count in SLOTS],
-        pairing, left_size, right_size, psi, own, right_env)
+        choice, [functools.partial(apply_call, count, planes, groups) for count in SLOTS],
+        plan, pairing, left_size, right_size, psi, own, right_env)
 
 
 def per_device(left_env, right_env, psi, pairing, left_size, right_size):

time: 91.5 us -> 86.1 us (0.941)
  other arithmetic: 3.36 us -> 0 us
  local copies, waits for them, and re-layouts: 2.4 us -> 1.18 us
    reduce_sum x8 -> x0, other arithmetic: 1.68 us -> none  [the longest x1 0.63 us: by_plane(): choice = jnp.sum(most > jnp.array(SLOTS[:-1]))]
    reduce_max x2 -> x0, other arithmetic: 1.35 us -> none  [the longest x1 0.71 us: by_plane(): jnp.max(jnp.sum(need_down, axis=1))]
    slice x1, local copies, waits for them, and re-layouts: 1.56 us -> 0.51 us  [by_plane(): choice += (plan[3, 0] > count).astype(jnp.int32)]
where the time goes in v2:
time: 86.1 us; the launch traced here: 84.5 us
  Pallas kernels  80.4 us (93%)
  between operations  2.67 us (3%)
  local copies, waits for them, and re-layouts  1.18 us (1%)
    pallas_call x1, Pallas kernels, apply_call(): pl.pallas_call(functools.partial(apply_kernel, count, planes, groups), ou...  57.5 us
    pallas_call x1, Pallas kernels, by_plane(): pl.pallas_call(functools.partial(spread_kernel, planes, groups), out_shap...  22.9 us

profile of v2, /device:TPU:0, one launch (start us, length us, event | category | flops | bytes accessed | tf_op | source)
XLA Modules:
  0.0 84.5 jit_solution(4835101396211356597)
XLA Ops:
  0.0 0.0 copy-start.1
  0.0 0.0 copy-start
  0.7 22.9 %spread.1 = (s32[8,128]{1,0:T(8,128)S(1)}, bf16[4,3,256,256]{3,2,1,0:T(8,128)(2,1)S(1)}) custom-call(s32[1,1]{1,0:T(1,128)S(6)} %copy.16.pairing, bf16[1,12,256,256]{3,2,1,0:T(8,128)(2,1)} %left_env.1), custom_call_target="tpu_custom_call" | custom-call | tf_op jit(solution)/shard_map/spread/pallas_call | solution.py:399
  23.6 0.5 slice.2
  26.1 0.0 copy-done.1
  26.1 0.0 copy-done
  26.1 57.8 %conditional.1 = (bf16[1,1,256,256]{3,2,1,0:T(8,128)(2,1)S(1)}) conditional(s32[]{:T(128)} %bitcast, (s32[8,128]{1,0:T(8,128)S(1)}, s32[1,1]{1,0:T(1,128)}, s32[16]{0:T(128)S(1)}, s32[1]{0:T(128)}, bf16[1,1,256,256]{3,2,1,0:T(8,128)(2,1)S(1)}, /*index=5*/bf16[4,3,256,256]{3,2,1,0:T(8,128)(2,1)S(1)}, ...), branch_computations={%region_0.0_spmd, %region_1.0_spmd, %region_2.0_spmd, %region_3.0_... | conditional | bytes 8 | solution.py:418
  26.1 57.5 %apply_3.1 = bf16[1,1,256,256]{3,2,1,0:T(8,128)(2,1)S(1)} custom-call(s32[8,128]{1,0:T(8,128)S(1)} %get-tuple-element.64.plan, s32[1,1]{1,0:T(1,128)} %get-tuple-element.66.pairing, s32[16]{0:T(128)S(1)} %get-tuple-element.68.left_size, s32[1]{0:T(128)} %get-tuple-element.69.right_size, bf16[1,1,256,256]{3,2,1,0:T(8,128)(2,1)S(1)} %get-tuple-element.70.psi, ...), custom_call_target="tpu_custom_call" | custom-call | tf_op jit(solution)/shard_map/cond/branch_0_fun/apply_3/pallas_call | solution.py:367
  83.9 0.7 copy.17
Async XLA Ops:
  0.0 26.1 %copy-start.1 = (s32[16]{0:T(128)S(1)}, s32[16]{0:T(128)}, u32[]{:S(2)}) copy-start(s32[16]{0:T(128)} %param.14) | copy-start | bytes 196
  0.0 26.1 %copy-start = (bf16[1,1,256,256]{3,2,1,0:T(8,128)(2,1)S(1)}, bf16[1,1,256,256]{3,2,1,0:T(8,128)(2,1)}, u32[]{:S(2)}) copy-start(bf16[1,1,256,256]{3,2,1,0:T(8,128)(2,1)} %param.12) | copy-start | bytes 393220
